TPU v7x, 32 devices: a whole 2x2x4 slice. The times are simulated.
32 devices in a mesh: groups: 2 (over x), feat: 8 (over z, y), store: 2 (over core).
Axes of the slice: x: 2, y: 2, z: 4, core: 2. Of those that a mesh axis runs over, the one named last changes fastest.
Arguments:
- activations: bfloat16 [6144, 8192], P(('groups', 'store'), 'feat'), parts along dimension 0, may hold values from -6 to 6
- output_grads: bfloat16 [6144, 8192], P(('groups', 'store'), 'feat'), parts along dimension 0, may hold values from -6 to 6
- input_basis: bfloat16 [8192, 64], P('feat'), may hold values from -0.0625 to 0.0625
- grad_basis: bfloat16 [8192, 64], P('feat'), may hold values from -0.0625 to 0.0625
- lengths: int32 [96], P(('groups', 'store')), parts along dimension 0, may hold values from 1 to 64, as said below
- stored_grads: bfloat16 [24576, 4096], P(('groups', 'feat', 'store')), parts along dimension 0, may hold values from -0.09375 to 0.09375
Outputs:
- scores: float32 [96, 12288], P('groups', ('feat', 'store')), parts along dimension 0
There are 2 independent parts, one for each index of `groups`. A program takes and returns all parts, laid end to end along the dimension named above; an argument that names none is the same for every part. Nothing has to cross between parts.
Inputs may be any that keep to these rules, and one draw needn't show every extreme that they name: `lengths`: every document has at least one live token; some document fills all 64 slots and some has one.
All inputs are finite; a program needn't handle non-finite values.
Results may differ from a plain program's by a relative error of at most 0.0029.
Values may be sent and summed in bfloat16 or wider, within the bound.
A program may use at most 64 MiB of HBM per device.

v0:
```python
import jax
import jax.numpy as jnp
from jax import lax
from jax.sharding import PartitionSpec as P

R = 64
TOKDOC = 64


def document_grads(summed, doc_lengths):
    count = doc_lengths.shape[0]
    blocks = summed.reshape(count, TOKDOC, 2 * R)
    position = lax.broadcasted_iota(jnp.int32, (count, TOKDOC, 1), 1)
    keeper = (position < doc_lengths[:, None, None]).astype(jnp.float32)
    grad_side = blocks[:, :, :R] * keeper
    input_side = blocks[:, :, R:]
    outer = jnp.einsum("ntr,nts->nrs", grad_side, input_side, precision=lax.Precision.HIGHEST)
    scaled = outer / doc_lengths.astype(jnp.float32)[:, None, None]
    return scaled.reshape(count, R * R).astype(jnp.bfloat16)


def per_device(activations, output_grads, input_basis, grad_basis, lengths, stored_grads):
    grad_proj = jnp.dot(output_grads, grad_basis, preferred_element_type=jnp.float32)
    input_proj = jnp.dot(activations, input_basis, preferred_element_type=jnp.float32)
    summed = lax.psum(jnp.concatenate([grad_proj, input_proj], axis=1), "feat")
    queries = document_grads(summed, lengths)
    return lax.dot_general(
        lax.all_gather(queries, "store", axis=0, tiled=True),
        stored_grads,
        (((1,), (1,)), ((), ())),
        preferred_element_type=jnp.float32,
    )


def solution(mesh):
    placed = (
        P(("groups", "store"), "feat"),
        P(("groups", "store"), "feat"),
        P("feat", None),
        P("feat", None),
        P(("groups", "store")),
        P(("groups", "feat", "store"), None),
    )
    return jax.shard_map(
        per_device,
        mesh=mesh,
        in_specs=placed,
        out_specs=P("groups", ("feat", "store")),
        check_vma=False,
    )
```

profile of v0, /device:TPU:0, one launch (start us, length us, event | category | flops | bytes accessed | tf_op | source)
XLA Modules:
  0.0 112.3 jit_solution(6969232429745797038)
XLA Ops:
  6.5 0.0 copy-start
  6.5 0.0 copy-start.2
  6.5 0.0 all-reduce.2.cloned.1.call-start
  6.5 1.9 %copy-done = bf16[1536,1024]{1,0:T(8,128)(2,1)S(1)} copy-done((bf16[1536,1024]{1,0:T(8,128)(2,1)S(1)}, bf16[1536,1024]{1,0:T(8,128)(2,1)}, u32[]{:S(2)}) %copy-start) | copy-done | bytes 3145752
  8.4 0.0 copy-start.1
  8.4 2.1 %fusion.4 = f32[1536,64]{0,1:T(8,128)S(1)} fusion(bf16[1536,1024]{1,0:T(8,128)(2,1)S(1)} %copy-done, bf16[1024,64]{0,1:T(8,128)(2,1)} %param.9), kind=kOutput, calls=%fused_computation.8 | convolution fusion | flops 201326592 | bytes 3670016 | tf_op jit(solution)/shard_map/dot_general | solution.py:23
  10.6 0.0 copy-done.2
  10.6 0.0 copy-done.1
  10.6 1.1 fusion.5
  11.6 0.0 copy-start.3
  11.7 0.9 pad_maximum_fusion
  12.6 2.3 %copy.9 = f32[1536,128]{1,0:T(8,128)} copy(f32[1536,128]{0,1:T(8,128)} %pad_maximum_fusion) | data formatting | bytes 1572864 | tf_op jit(solution)/shard_map/concatenate | solution.py:25
  14.9 0.0 all-reduce.2.cloned.1.call-update
  14.9 0.0 copy-done.3
  14.9 0.1 fusion.3
  15.0 77.5 %all-reduce.2.cloned.1.call-done = f32[24,64,128]{2,1,0:T(8,128)} async-done(((f32[24,64,128]{2,1,0:T(8,128)}), f32[24,64,128]{2,1,0:T(8,128)}) %all-reduce.2.cloned.1.call-update) | async-done | bytes 786448 | tf_op jit(solution)/shard_map/psum | solution.py:25
  92.5 4.0 %fusion = bf16[24,64,64]{2,1,0:T(8,128)(2,1)} fusion(f32[24,64,128]{2,1,0:T(8,128)} %all-reduce.2.cloned.1.call-done, f32[24]{0:T(128)S(1)} %convert_element_type.18, f32[24,64]{1,0:T(8,128)S(1)} %fusion.3), kind=kOutput, calls=%fused_computation.1 | convolution fusion | flops 75792384 | bytes 1775712 | tf_op jit(solution)/shard_map/ntr,nts->nrs/dot_general | solution.py:17
  96.5 1.4 %convert_element_type.20 = bf16[24,4096]{1,0:T(8,128)(2,1)S(1)} reshape(bf16[24,64,64]{2,1,0:T(8,128)(2,1)} %fusion) | data formatting | bytes 393216 | tf_op jit(solution)/shard_map/convert_element_type | solution.py:19
  97.9 2.1 %all_gather.3 = bf16[48,4096]{1,0:T(8,128)(2,1)S(1)} all-gather(bf16[24,4096]{1,0:T(8,128)(2,1)S(1)} %convert_element_type.20), channel_id=1, replica_groups=mesh['groups'=2,'feat'=8,'store'=2] {'store'}, dimensions={0}, use_global_device_ids=true | all-gather | bytes 589824 | tf_op jit(solution)/shard_map/all_gather | solution.py:28
  100.0 5.5 %fusion.6 = f32[48,768]{1,0:T(8,128)} fusion(bf16[48,4096]{1,0:T(8,128)(2,1)S(1)} %all_gather.3, bf16[768,4096]{1,0:T(8,128)(2,1)} %param.11), kind=kOutput, calls=%fused_computation.10 | convolution fusion | flops 301989888 | bytes 6832128 | tf_op jit(solution)/shard_map/dot_general | solution.py:27
  (1 shorter events, 0.0 us)
Async XLA Ops:
  6.5 1.9 %copy-start = (bf16[1536,1024]{1,0:T(8,128)(2,1)S(1)}, bf16[1536,1024]{1,0:T(8,128)(2,1)}, u32[]{:S(2)}) copy-start(bf16[1536,1024]{1,0:T(8,128)(2,1)} %param.7) | copy-start | bytes 9437188
  6.5 4.0 %copy-start.2 = (bf16[1024,64]{0,1:T(8,128)(2,1)S(1)}, bf16[1024,64]{0,1:T(8,128)(2,1)}, u32[]{:S(2)}) copy-start(bf16[1024,64]{0,1:T(8,128)(2,1)} %param.8) | copy-start | bytes 393220
  6.5 86.0 %all-reduce.2.cloned.1.call-start = ((), (), s32[]{:S(2)}) async-start(), calls=%async_computation | async-start | bytes 1572864 | tf_op jit(solution)/shard_map/psum | solution.py:25
  8.4 2.1 %copy-start.1 = (bf16[1536,1024]{1,0:T(8,128)(2,1)S(1)}, bf16[1536,1024]{1,0:T(8,128)(2,1)}, u32[]{:S(2)}) copy-start(bf16[1536,1024]{1,0:T(8,128)(2,1)} %param.6) | copy-start | bytes 9437188
  11.6 3.3 %copy-start.3 = (s32[24]{0:T(128)S(1)}, s32[24]{0:T(128)}, u32[]{:S(2)}) copy-start(s32[24]{0:T(128)} %param.10) | copy-start | bytes 292
Sparse Core Ops, SparseCore 0:
  15.0 77.4 all-reduce.1
where the time goes:
time: 113 us; the launch traced here: 112 us
  waiting for transfers between devices  77.5 us (69%)
  between operations  13.4 us (12%)
  matrix products  12.6 us (11%)
  local copies, waits for them, and re-layouts  5.56 us (5%)
  blocking collectives  2.09 us (2%)
    psum x1, waiting for transfers between devices, per_device(): summed = lax.psum(jnp.concatenate([grad_proj, input_proj], axis=1), 'feat')  77.5 us
    dot_general x1, matrix products, per_device(): lax.dot_general(lax.all_gather(queries, 'store', axis=0, tiled=True), sto...  5.46 us
    dot_general x1, matrix products, document_grads(): jnp.einsum('ntr,nts->nrs', grad_side, input_side, precision=lax.Precision...  3.98 us
    concatenate x1, local copies, waits for them, and re-layouts, per_device(): summed = lax.psum(jnp.concatenate([grad_proj, input_proj], axis=1), 'feat')  2.3 us
  transfers between devices with their start and end apart: 1, of which 1 were waited for; matrix products, arithmetic and copies ran while one was open for 0% of the time, Pallas kernels for 0%

commit v1 on v0

v1 whole, which is shorter than its diff:
```python
import functools

import jax
import jax.numpy as jnp
from jax import lax
from jax.experimental import pallas as pl
from jax.experimental.pallas import tpu as pltpu
from jax.sharding import PartitionSpec as P

MESH = pl.DeviceIdType.MESH
PAIR = 2
HALVES = 2
LANES = 128


def remote(src, dst, send_sem, recv_sem, target):
    return pltpu.make_async_remote_copy(
        src_ref=src, dst_ref=dst, send_sem=send_sem, recv_sem=recv_sem, device_id=target, device_id_type=MESH
    )


def kernel(
    feat, stores, slots_per_doc,
    acts, grads, in_basis, grad_basis, lengths, stored, scores,
    acts_v, grads_v, in_basis_v, grad_basis_v, stored_v, partial,
    pair_out, pair_in, line_out, line_in, gathered, wide, queries,
    acts_sem, grads_sem, basis_sem, stored_sem,
    pair_send, pair_recv, line_send, line_recv, all_send, all_recv, core_send, core_recv,
):
    line = feat // PAIR
    block = acts_v.shape[1] // PAIR
    docs = block // slots_per_doc
    rank = in_basis.shape[1]
    pairs = rank * rank // LANES
    part_rows = pairs // HALVES
    order = list(range(1, line)) + [0]

    me = lax.axis_index("feat")
    core = lax.axis_index("store")
    my_line, my_pair = me // PAIR, lax.rem(me, PAIR)
    other = 1 - my_pair
    twin = my_line * PAIR + other

    basis_loads = [
        pltpu.make_async_copy(in_basis, in_basis_v, basis_sem.at[0]),
        pltpu.make_async_copy(grad_basis, grad_basis_v, basis_sem.at[1]),
    ]
    for load in basis_loads:
        load.start()
    loads = {}
    for step in order:
        spot = lax.rem(my_line + step, line)
        rows = pl.ds(pl.multiple_of(spot * (PAIR * block), PAIR * block), PAIR * block)
        loads[step] = [
            pltpu.make_async_copy(acts.at[rows], acts_v.at[step], acts_sem.at[step]),
            pltpu.make_async_copy(grads.at[rows], grads_v.at[step], grads_sem.at[step]),
        ]
        for load in loads[step]:
            load.start()

    barrier = pltpu.get_barrier_semaphore()
    for shift in range(1, feat):
        pl.semaphore_signal(barrier, inc=1, device_id={"feat": lax.rem(me + shift, feat)}, device_id_type=MESH)
    for shift in range(1, stores):
        pl.semaphore_signal(barrier, inc=1, device_id={"store": lax.rem(core + shift, stores)}, device_id_type=MESH)

    row = lax.broadcasted_iota(jnp.int32, (rank, LANES), 0)
    lane = lax.broadcasted_iota(jnp.int32, (rank, LANES), 1)
    grad_place = (lane == (row % 2) * (rank // 2) + row // 2).astype(jnp.bfloat16)
    in_place = (lane == row + rank).astype(jnp.bfloat16)
    for load in basis_loads:
        load.wait()
    in_wide = jnp.dot(in_basis_v[...], in_place, preferred_element_type=jnp.float32).astype(jnp.bfloat16)
    grad_wide = jnp.dot(grad_basis_v[...], grad_place, preferred_element_type=jnp.float32).astype(jnp.bfloat16)

    pair_copies = {}
    for index, step in enumerate(order):
        for load in loads[step]:
            load.wait()
        partial[step] = jnp.dot(acts_v[step], in_wide, preferred_element_type=jnp.float32) + jnp.dot(
            grads_v[step], grad_wide, preferred_element_type=jnp.float32
        )
        theirs = pl.ds(pl.multiple_of(other * block, block), block)
        pair_out[step] = partial[step, theirs, :]
        if index == 0:
            pl.semaphore_wait(barrier, feat - 1 + stores - 1)
        pair_copies[step] = remote(
            pair_out.at[step], pair_in.at[step], pair_send.at[step], pair_recv.at[step], {"feat": twin}
        )
        pair_copies[step].start()

    half = stored.shape[1] // HALVES
    stored_loads = []
    for part in range(HALVES):
        columns = pl.ds(part * half, half)
        load = pltpu.make_async_copy(stored.at[:, columns], stored_v.at[part], stored_sem.at[part])
        load.start()
        stored_loads.append(load)

    mine = pl.ds(pl.multiple_of(my_pair * block, block), block)
    line_copies = {}
    total = None
    for step in order:
        pair_copies[step].wait_recv()
        both = partial[step, mine, :] + pair_in[step]
        if step == 0:
            total = both
        else:
            line_out[step] = both
            spot = lax.rem(my_line + step, line)
            line_copies[step] = remote(
                line_out.at[step], line_in.at[step], line_send.at[step], line_recv.at[step],
                {"feat": spot * PAIR + my_pair},
            )
            line_copies[step].start()
    for step in order[:-1]:
        line_copies[step].wait_recv()
        total = total + line_in[step]

    position = lax.broadcasted_iota(jnp.int32, (slots_per_doc, rank), 0)
    left = lax.broadcasted_iota(jnp.int32, (slots_per_doc, LANES), 1) < rank
    slot = core * feat + me
    for doc in range(docs):
        length = lengths[me * docs + doc]
        rows = total[doc * slots_per_doc:(doc + 1) * slots_per_doc]
        grad_side = jnp.where(position < length, rows[:, :rank], 0.0)
        in_side = jnp.where(left, pltpu.roll(rows, rank, 1), rows)
        outer = lax.dot_general(
            grad_side, in_side, (((0,), (0,)), ((), ())),
            precision=lax.Precision.HIGHEST, preferred_element_type=jnp.float32,
        )
        query = jnp.where(left[:pairs], outer[:pairs], outer[pairs:]) / length.astype(jnp.float32)
        query = query.astype(jnp.bfloat16)
        for part in range(HALVES):
            gathered[part, slot, pl.ds(doc * part_rows, part_rows), :] = query[part * part_rows:(part + 1) * part_rows]

    sent = []
    for part in range(HALVES):
        own = gathered.at[part, slot]
        for shift in range(1, stores):
            sent.append(remote(
                own, own, core_send.at[part, shift, 0], core_recv.at[part, shift, 0],
                {"store": lax.rem(core + shift, stores)},
            ))
            sent[-1].start()
        for shift in range(1, feat):
            sent.append(remote(
                own, own, all_send.at[part, shift], all_recv.at[part, shift], {"feat": lax.rem(me + shift, feat)}
            ))
            sent[-1].start()

    wide_rows = wide.shape[0]
    all_docs = queries.shape[0]
    tile = 256
    for part in range(HALVES):
        for shift in range(1, feat):
            source = core * feat + lax.rem(me + feat - shift, feat)
            there = gathered.at[part, source]
            remote(
                there, there, all_send.at[part, shift], all_recv.at[part, shift], {"feat": lax.rem(me + shift, feat)}
            ).wait_recv()
            for hop in range(1, stores):
                sent.append(remote(
                    there, there, core_send.at[part, hop, shift], core_recv.at[part, hop, shift],
                    {"store": lax.rem(core + hop, stores)},
                ))
                sent[-1].start()
        for hop in range(1, stores):
            from_core = lax.rem(core + stores - hop, stores)
            for shift in range(feat):
                there = gathered.at[part, from_core * feat + lax.rem(me + feat - shift, feat)]
                remote(
                    there, there, core_send.at[part, hop, shift], core_recv.at[part, hop, shift],
                    {"store": lax.rem(core + hop, stores)},
                ).wait_recv()
        wide[...] = gathered[part].reshape(wide_rows, LANES).astype(jnp.float32)
        for pair in range(part_rows):
            queries[:, pair * LANES:(pair + 1) * LANES] = wide[pl.ds(pair, all_docs, part_rows), :].astype(jnp.bfloat16)
        stored_loads[part].wait()
        for start in range(0, stored.shape[0], tile):
            product = lax.dot_general(
                queries[...], stored_v[part, start:start + tile, :], (((1,), (1,)), ((), ())),
                preferred_element_type=jnp.float32,
            )
            if part == 0:
                scores[:, start:start + tile] = product
            else:
                scores[:, start:start + tile] += product

    for step in order:
        pair_copies[step].wait_send()
        if step:
            line_copies[step].wait_send()
    for copy in sent:
        copy.wait_send()


def per_device(feat, stores, activations, output_grads, input_basis, grad_basis, lengths, stored_grads):
    tokens, features = activations.shape
    slots_per_doc = tokens // lengths.shape[0]
    rank = input_basis.shape[1]
    rows, depth = stored_grads.shape
    docs = lengths.shape[0] * stores
    line = feat // PAIR
    block = tokens // feat
    part_rows = rank * rank // LANES // HALVES
    share = block // slots_per_doc * part_rows
    bf16, f32 = jnp.bfloat16, jnp.float32
    dma = pltpu.SemaphoreType.DMA
    anywhere = pl.BlockSpec(memory_space=pl.ANY)
    return pl.pallas_call(
        functools.partial(kernel, feat, stores, slots_per_doc),
        out_shape=jax.ShapeDtypeStruct((docs, rows), f32),
        in_specs=[anywhere] * 4 + [pl.BlockSpec(memory_space=pltpu.SMEM), anywhere],
        out_specs=pl.BlockSpec(memory_space=pltpu.VMEM),
        scratch_shapes=[
            pltpu.VMEM((line, PAIR * block, features), bf16),
            pltpu.VMEM((line, PAIR * block, features), bf16),
            pltpu.VMEM((features, rank), bf16),
            pltpu.VMEM((features, rank), bf16),
            pltpu.VMEM((HALVES, rows, depth // HALVES), bf16),
            pltpu.VMEM((line, PAIR * block, LANES), f32),
            pltpu.VMEM((line, block, LANES), f32),
            pltpu.VMEM((line, block, LANES), f32),
            pltpu.VMEM((line, block, LANES), f32),
            pltpu.VMEM((line, block, LANES), f32),
            pltpu.VMEM((HALVES, stores * feat, share, LANES), bf16),
            pltpu.VMEM((docs * part_rows, LANES), f32),
            pltpu.VMEM((docs, depth // HALVES), bf16),
            dma((line,)), dma((line,)), dma((2,)), dma((HALVES,)),
            dma((line,)), dma((line,)), dma((line,)), dma((line,)),
            dma((HALVES, feat)), dma((HALVES, feat)),
            dma((HALVES, stores, feat)), dma((HALVES, stores, feat)),
        ],
        compiler_params=pltpu.CompilerParams(
            collective_id=0, has_side_effects=True, vmem_limit_bytes=56 * 1024 * 1024
        ),
        cost_estimate=pl.CostEstimate(
            flops=4 * tokens * features * rank + 2 * docs * rows * depth,
            bytes_accessed=4 * tokens * features + 2 * rows * depth + 4 * docs * rows,
            transcendentals=0,
        ),
    )(activations, output_grads, input_basis, grad_basis, lengths, stored_grads)


def solution(mesh):
    placed = (
        P(("groups", "store"), "feat"),
        P(("groups", "store"), "feat"),
        P("feat", None),
        P("feat", None),
        P(("groups", "store")),
        P(("groups", "feat", "store"), None),
    )
    return jax.shard_map(
        functools.partial(per_device, mesh.shape["feat"], mesh.shape["store"]),
        mesh=mesh,
        in_specs=placed,
        out_specs=P("groups", ("feat", "store")),
        check_vma=False,
    )
```

time: 113 us -> 38.1 us (0.34)
  waiting for transfers between devices: 77.5 us -> 0 us
  Pallas kernels: 0 us -> 32.9 us
  between operations: 13.4 us -> 0.01 us
  matrix products: 12.6 us -> 0 us
  blocking collectives: 2.09 us -> 0 us
    psum x1 -> x0, waiting for transfers between devices: 77.5 us -> none  [per_device(): summed = lax.psum(jnp.concatenate([grad_proj, input_proj], axis=1), 'feat')]
    pallas_call x0 -> x1, Pallas kernels: none -> 32.9 us  [per_device(): pl.pallas_call(functools.partial(kernel, feat, stores, slots_per_doc), ou...]
    dot_general x4 -> x0, matrix products: 12.6 us -> none  [the longest x1 5.46 us: per_device(): lax.dot_general(lax.all_gather(queries, 'store', axis=0, tiled=True), sto...]
    unnamed x8 -> x3, local copies, waits for them, and re-layouts: 1.9 us -> 5.05 us
    concatenate x1 -> x0, local copies, waits for them, and re-layouts: 2.3 us -> none  [per_device(): summed = lax.psum(jnp.concatenate([grad_proj, input_proj], axis=1), 'feat')]
    all_gather x1 -> x0, blocking collectives: 2.09 us -> none  [per_device(): lax.all_gather(queries, 'store', axis=0, tiled=True)]
    convert_element_type x1 -> x0, local copies, waits for them, and re-layouts: 1.36 us -> none  [document_grads(): return scaled.reshape(count, R * R).astype(jnp.bfloat16)]
  transfers between devices with their start and end apart: 1 -> 0, of which waited for: 1 -> 0; matrix products, arithmetic and copies ran while one was open for 0% -> 0% of each run, Pallas kernels for 0% -> 0%
where the time goes in v1:
time: 38.1 us; the launch traced here: 38 us
  Pallas kernels  32.9 us (86%)
  local copies, waits for them, and re-layouts  5.05 us (13%)
    pallas_call x1, Pallas kernels, per_device(): pl.pallas_call(functools.partial(kernel, feat, stores, slots_per_doc), ou...  32.9 us
    unnamed x3, local copies, waits for them, and re-layouts  5.05 us

profile of v1, /device:TPU:0, one launch (start us, length us, event | category | flops | bytes accessed | tf_op | source)
XLA Modules:
  0.0 38.0 jit_solution(10766646806661512490)
XLA Ops:
  0.0 1.7 %copy.7.in_basis = bf16[1024,64]{1,0:T(8,128)(2,1)} copy(bf16[1024,64]{0,1:T(8,128)(2,1)} %param.8) | data formatting | bytes 262144 | tf_op args[2]
  1.7 1.7 %copy.8.grad_basis = bf16[1024,64]{1,0:T(8,128)(2,1)} copy(bf16[1024,64]{0,1:T(8,128)(2,1)} %param.9) | data formatting | bytes 262144 | tf_op args[3]
  3.5 32.9 %shard_map.64 = f32[48,768]{1,0:T(8,128)} custom-call(bf16[1536,1024]{1,0:T(8,128)(2,1)} %acts.1, bf16[1536,1024]{1,0:T(8,128)(2,1)} %grads.1, bf16[1024,64]{1,0:T(8,128)(2,1)} %copy.7.in_basis, bf16[1024,64]{1,0:T(8,128)(2,1)} %copy.8.grad_basis, s32[24]{0:T(128)} %lengths.1, bf16[768,4096]{1,0:T(8,128)(2,1)} %stored.1), custom_call_target="tpu_custom_call" | custom-call | flops 704643072 | bytes 12730368 | tf_op jit(solution)/shard_map/pallas_call | solution.py:211
  36.4 1.6 %copy.10 = f32[48,768]{1,0:T(8,128)} copy(f32[48,768]{1,0:T(8,128)} %shard_map.64) | data formatting | bytes 294912

commit v2 on v1

--- a/solution.py
+++ b/solution.py
@@ -11,12 +11,28 @@
 PAIR = 2
 HALVES = 2
 LANES = 128
+HEADER = 16
 
 
 def remote(src, dst, send_sem, recv_sem, target):
     return pltpu.make_async_remote_copy(
         src_ref=src, dst_ref=dst, send_sem=send_sem, recv_sem=recv_sem, device_id=target, device_id_type=MESH
     )
+
+
+def encode(ref, values):
+    block = values.shape[0]
+    top = jnp.max(jnp.abs(values), axis=0, keepdims=True)
+    power = 14.0 - jnp.floor(jnp.log2(jnp.maximum(top, 1e-30)))
+    scaled = jnp.clip(jnp.round(values * jnp.exp2(power)), -32767.0, 32767.0)
+    ref[:block] = scaled.astype(jnp.int32).astype(jnp.int16)
+    ref[block:] = jnp.broadcast_to(power, (ref.shape[0] - block, LANES)).astype(jnp.int32).astype(jnp.int16)
+
+
+def decode(ref, block):
+    values = ref[:block].astype(jnp.int32).astype(jnp.float32)
+    power = ref[block:].astype(jnp.int32).astype(jnp.float32)[:1]
+    return values * jnp.exp2(-power)
 
 
 def kernel(
@@ -30,7 +46,7 @@
     line = feat // PAIR
     block = acts_v.shape[1] // PAIR
     docs = block // slots_per_doc
-    rank = in_basis.shape[1]
+    rank = in_basis.shape[0]
     pairs = rank * rank // LANES
     part_rows = pairs // HALVES
     order = list(range(1, line)) + [0]
@@ -70,8 +86,10 @@
     in_place = (lane == row + rank).astype(jnp.bfloat16)
     for load in basis_loads:
         load.wait()
-    in_wide = jnp.dot(in_basis_v[...], in_place, preferred_element_type=jnp.float32).astype(jnp.bfloat16)
-    grad_wide = jnp.dot(grad_basis_v[...], grad_place, preferred_element_type=jnp.float32).astype(jnp.bfloat16)
+    over_rank = (((0,), (0,)), ((), ()))
+    in_wide = lax.dot_general(in_basis_v[...], in_place, over_rank, preferred_element_type=jnp.float32)
+    grad_wide = lax.dot_general(grad_basis_v[...], grad_place, over_rank, preferred_element_type=jnp.float32)
+    in_wide, grad_wide = in_wide.astype(jnp.bfloat16), grad_wide.astype(jnp.bfloat16)
 
     pair_copies = {}
     for index, step in enumerate(order):
@@ -81,7 +99,7 @@
             grads_v[step], grad_wide, preferred_element_type=jnp.float32
         )
         theirs = pl.ds(pl.multiple_of(other * block, block), block)
-        pair_out[step] = partial[step, theirs, :]
+        encode(pair_out.at[step], partial[step, theirs, :])
         if index == 0:
             pl.semaphore_wait(barrier, feat - 1 + stores - 1)
         pair_copies[step] = remote(
@@ -102,11 +120,11 @@
     total = None
     for step in order:
         pair_copies[step].wait_recv()
-        both = partial[step, mine, :] + pair_in[step]
+        both = partial[step, mine, :] + decode(pair_in.at[step], block)
         if step == 0:
             total = both
         else:
-            line_out[step] = both
+            encode(line_out.at[step], both)
             spot = lax.rem(my_line + step, line)
             line_copies[step] = remote(
                 line_out.at[step], line_in.at[step], line_send.at[step], line_recv.at[step],
@@ -115,7 +133,7 @@
             line_copies[step].start()
     for step in order[:-1]:
         line_copies[step].wait_recv()
-        total = total + line_in[step]
+        total = total + decode(line_in.at[step], block)
 
     position = lax.broadcasted_iota(jnp.int32, (slots_per_doc, rank), 0)
     left = lax.broadcasted_iota(jnp.int32, (slots_per_doc, LANES), 1) < rank
@@ -216,14 +234,14 @@
         scratch_shapes=[
             pltpu.VMEM((line, PAIR * block, features), bf16),
             pltpu.VMEM((line, PAIR * block, features), bf16),
-            pltpu.VMEM((features, rank), bf16),
-            pltpu.VMEM((features, rank), bf16),
+            pltpu.VMEM((rank, features), bf16),
+            pltpu.VMEM((rank, features), bf16),
             pltpu.VMEM((HALVES, rows, depth // HALVES), bf16),
             pltpu.VMEM((line, PAIR * block, LANES), f32),
-            pltpu.VMEM((line, block, LANES), f32),
-            pltpu.VMEM((line, block, LANES), f32),
-            pltpu.VMEM((line, block, LANES), f32),
-            pltpu.VMEM((line, block, LANES), f32),
+            pltpu.VMEM((line, block + HEADER, LANES), jnp.int16),
+            pltpu.VMEM((line, block + HEADER, LANES), jnp.int16),
+            pltpu.VMEM((line, block + HEADER, LANES), jnp.int16),
+            pltpu.VMEM((line, block + HEADER, LANES), jnp.int16),
             pltpu.VMEM((HALVES, stores * feat, share, LANES), bf16),
             pltpu.VMEM((docs * part_rows, LANES), f32),
             pltpu.VMEM((docs, depth // HALVES), bf16),
@@ -240,7 +258,7 @@
             bytes_accessed=4 * tokens * features + 2 * rows * depth + 4 * docs * rows,
             transcendentals=0,
         ),
-    )(activations, output_grads, input_basis, grad_basis, lengths, stored_grads)
+    )(activations, output_grads, input_basis.T, grad_basis.T, lengths, stored_grads)
 
 
 def solution(mesh):

time: 38.1 us -> 29.6 us (0.78)
  Pallas kernels: 32.9 us -> 27.8 us
  local copies, waits for them, and re-layouts: 5.05 us -> 1.58 us
    pallas_call x1, Pallas kernels: 32.9 us -> 27.8 us  [per_device(): pl.pallas_call(functools.partial(kernel, feat, stores, slots_per_doc), ou...]
    unnamed x3 -> x1, local copies, waits for them, and re-layouts: 5.05 us -> 1.58 us
where the time goes in v2:
time: 29.6 us; the launch traced here: 29.4 us
  Pallas kernels  27.8 us (94%)
  local copies, waits for them, and re-layouts  1.58 us (5%)
    pallas_call x1, Pallas kernels, per_device(): pl.pallas_call(functools.partial(kernel, feat, stores, slots_per_doc), ou...  27.8 us
    unnamed x1, local copies, waits for them, and re-layouts  1.58 us

profile of v2, /device:TPU:0, one launch (start us, length us, event | category | flops | bytes accessed | tf_op | source)
XLA Modules:
  0.0 29.4 jit_solution(3217953524301919569)
XLA Ops:
  0.0 27.8 %shard_map.64 = f32[48,768]{1,0:T(8,128)} custom-call(bf16[1536,1024]{1,0:T(8,128)(2,1)} %acts.1, bf16[1536,1024]{1,0:T(8,128)(2,1)} %grads.1, bf16[64,1024]{1,0:T(8,128)(2,1)} %bitcast.2, bf16[64,1024]{1,0:T(8,128)(2,1)} %bitcast.3, s32[24]{0:T(128)} %lengths.1, bf16[768,4096]{1,0:T(8,128)(2,1)} %stored.1), custom_call_target="tpu_custom_call" | custom-call | flops 704643072 | bytes 12730368 | tf_op jit(solution)/shard_map/pallas_call | solution.py:229
  27.8 1.6 %copy.8 = f32[48,768]{1,0:T(8,128)} copy(f32[48,768]{1,0:T(8,128)} %shard_map.64) | data formatting | bytes 294912

commit v3 on v2

--- a/solution.py
+++ b/solution.py
@@ -41,7 +41,7 @@
     acts_v, grads_v, in_basis_v, grad_basis_v, stored_v, partial,
     pair_out, pair_in, line_out, line_in, gathered, wide, queries,
     acts_sem, grads_sem, basis_sem, stored_sem,
-    pair_send, pair_recv, line_send, line_recv, all_send, all_recv, core_send, core_recv,
+    pair_send, pair_recv, line_send, line_recv, all_send, all_recv, twin_send, twin_recv, core_send, core_recv,
 ):
     line = feat // PAIR
     block = acts_v.shape[1] // PAIR
@@ -75,10 +75,11 @@
             load.start()
 
     barrier = pltpu.get_barrier_semaphore()
-    for shift in range(1, feat):
-        pl.semaphore_signal(barrier, inc=1, device_id={"feat": lax.rem(me + shift, feat)}, device_id_type=MESH)
-    for shift in range(1, stores):
-        pl.semaphore_signal(barrier, inc=1, device_id={"store": lax.rem(core + shift, stores)}, device_id_type=MESH)
+    partners = [{"feat": twin}]
+    partners += [{"feat": lax.rem(my_line + shift, line) * PAIR + my_pair} for shift in range(1, line)]
+    partners += [{"store": lax.rem(core + shift, stores)} for shift in range(1, stores)]
+    for partner in partners:
+        pl.semaphore_signal(barrier, inc=1, device_id=partner, device_id_type=MESH)
 
     row = lax.broadcasted_iota(jnp.int32, (rank, LANES), 0)
     lane = lax.broadcasted_iota(jnp.int32, (rank, LANES), 1)
@@ -101,7 +102,7 @@
         theirs = pl.ds(pl.multiple_of(other * block, block), block)
         encode(pair_out.at[step], partial[step, theirs, :])
         if index == 0:
-            pl.semaphore_wait(barrier, feat - 1 + stores - 1)
+            pl.semaphore_wait(barrier, len(partners))
         pair_copies[step] = remote(
             pair_out.at[step], pair_in.at[step], pair_send.at[step], pair_recv.at[step], {"feat": twin}
         )
@@ -137,7 +138,6 @@
 
     position = lax.broadcasted_iota(jnp.int32, (slots_per_doc, rank), 0)
     left = lax.broadcasted_iota(jnp.int32, (slots_per_doc, LANES), 1) < rank
-    slot = core * feat + me
     for doc in range(docs):
         length = lengths[me * docs + doc]
         rows = total[doc * slots_per_doc:(doc + 1) * slots_per_doc]
@@ -150,48 +150,74 @@
         query = jnp.where(left[:pairs], outer[:pairs], outer[pairs:]) / length.astype(jnp.float32)
         query = query.astype(jnp.bfloat16)
         for part in range(HALVES):
-            gathered[part, slot, pl.ds(doc * part_rows, part_rows), :] = query[part * part_rows:(part + 1) * part_rows]
+            gathered[part, core, my_pair, my_line, pl.ds(doc * part_rows, part_rows), :] = query[part * part_rows:(part + 1) * part_rows]
 
     sent = []
+
+    def send(*copy):
+        sent.append(remote(*copy))
+        sent[-1].start()
+
+    def share(part, source, hop):
+        for shift in range(1, stores):
+            send(
+                gathered.at[part, core, source], gathered.at[part, core, source],
+                core_send.at[part, shift, hop], core_recv.at[part, shift, hop],
+                {"store": lax.rem(core + shift, stores)},
+            )
+
+    def to_twin(part, spot, shift):
+        there = gathered.at[part, core, my_pair, spot]
+        send(there, there, twin_send.at[part, shift], twin_recv.at[part, shift], {"feat": twin})
+
+    def along_line(part):
+        for shift in range(1, line):
+            source = lax.rem(my_line + line - shift, line)
+            there = gathered.at[part, core, my_pair, source]
+            remote(
+                there, there, all_send.at[part, shift], all_recv.at[part, shift], {"feat": twin}
+            ).wait_recv()
+            to_twin(part, source, shift)
+        share(part, my_pair, 0)
+
+    def from_twin(part):
+        for shift in range(line):
+            there = gathered.at[part, core, other, lax.rem(my_line + line - shift, line)]
+            remote(
+                there, there, twin_send.at[part, shift], twin_recv.at[part, shift], {"feat": twin}
+            ).wait_recv()
+        share(part, other, 1)
+
+    def from_cores(part):
+        for shift in range(1, stores):
+            for hop, source in enumerate((my_pair, other)):
+                there = gathered.at[part, lax.rem(core + stores - shift, stores), source]
+                remote(
+                    there, there, core_send.at[part, shift, hop], core_recv.at[part, shift, hop],
+                    {"store": lax.rem(core + shift, stores)},
+                ).wait_recv()
+
     for part in range(HALVES):
-        own = gathered.at[part, slot]
-        for shift in range(1, stores):
-            sent.append(remote(
-                own, own, core_send.at[part, shift, 0], core_recv.at[part, shift, 0],
-                {"store": lax.rem(core + shift, stores)},
-            ))
-            sent[-1].start()
-        for shift in range(1, feat):
-            sent.append(remote(
-                own, own, all_send.at[part, shift], all_recv.at[part, shift], {"feat": lax.rem(me + shift, feat)}
-            ))
-            sent[-1].start()
+        own = gathered.at[part, core, my_pair, my_line]
+        for shift in range(1, line):
+            send(
+                own, own, all_send.at[part, shift], all_recv.at[part, shift],
+                {"feat": lax.rem(my_line + shift, line) * PAIR + my_pair},
+            )
+        to_twin(part, my_line, 0)
+    along_line(0)
+    from_twin(0)
 
     wide_rows = wide.shape[0]
     all_docs = queries.shape[0]
     tile = 256
     for part in range(HALVES):
-        for shift in range(1, feat):
-            source = core * feat + lax.rem(me + feat - shift, feat)
-            there = gathered.at[part, source]
-            remote(
-                there, there, all_send.at[part, shift], all_recv.at[part, shift], {"feat": lax.rem(me + shift, feat)}
-            ).wait_recv()
-            for hop in range(1, stores):
-                sent.append(remote(
-                    there, there, core_send.at[part, hop, shift], core_recv.at[part, hop, shift],
-                    {"store": lax.rem(core + hop, stores)},
-                ))
-                sent[-1].start()
-        for hop in range(1, stores):
-            from_core = lax.rem(core + stores - hop, stores)
-            for shift in range(feat):
-                there = gathered.at[part, from_core * feat + lax.rem(me + feat - shift, feat)]
-                remote(
-                    there, there, core_send.at[part, hop, shift], core_recv.at[part, hop, shift],
-                    {"store": lax.rem(core + hop, stores)},
-                ).wait_recv()
-        wide[...] = gathered[part].reshape(wide_rows, LANES).astype(jnp.float32)
+        if part + 1 < HALVES:
+            along_line(part + 1)
+        from_cores(part)
+        wide[...] = jnp.concatenate(
+            [gathered[part, c, f % PAIR, f // PAIR] for c in range(stores) for f in range(feat)]
+        ).astype(jnp.float32)
         for pair in range(part_rows):
             queries[:, pair * LANES:(pair + 1) * LANES] = wide[pl.ds(pair, all_docs, part_rows), :].astype(jnp.bfloat16)
         stored_loads[part].wait()
@@ -204,6 +230,8 @@
                 scores[:, start:start + tile] = product
             else:
                 scores[:, start:start + tile] += product
+        if part + 1 < HALVES:
+            from_twin(part + 1)
 
     for step in order:
         pair_copies[step].wait_send()
@@ -242,13 +270,13 @@
             pltpu.VMEM((line, block + HEADER, LANES), jnp.int16),
             pltpu.VMEM((line, block + HEADER, LANES), jnp.int16),
             pltpu.VMEM((line, block + HEADER, LANES), jnp.int16),
-            pltpu.VMEM((HALVES, stores * feat, share, LANES), bf16),
+            pltpu.VMEM((HALVES, stores, PAIR, line, share, LANES), bf16),
             pltpu.VMEM((docs * part_rows, LANES), f32),
             pltpu.VMEM((docs, depth // HALVES), bf16),
             dma((line,)), dma((line,)), dma((2,)), dma((HALVES,)),
             dma((line,)), dma((line,)), dma((line,)), dma((line,)),
-            dma((HALVES, feat)), dma((HALVES, feat)),
-            dma((HALVES, stores, feat)), dma((HALVES, stores, feat)),
+            dma((HALVES, line)), dma((HALVES, line)), dma((HALVES, line)), dma((HALVES, line)),
+            dma((HALVES, stores, PAIR)), dma((HALVES, stores, PAIR)),
         ],
         compiler_params=pltpu.CompilerParams(
             collective_id=0, has_side_effects=True, vmem_limit_bytes=56 * 1024 * 1024

time: 29.6 us -> 32.1 us (1.084)
  the two profiles are of different devices: /device:TPU:0 before, /device:TPU:1 now
where the time goes in v3:
time: 32.1 us; the launch traced here: 31.9 us
  Pallas kernels  30.4 us (95%)
  local copies, waits for them, and re-layouts  1.58 us (5%)
    pallas_call x1, Pallas kernels, per_device(): pl.pallas_call(functools.partial(kernel, feat, stores, slots_per_doc), ou...  30.4 us
    unnamed x1, local copies, waits for them, and re-layouts  1.58 us

profile of v3, /device:TPU:1, one launch (start us, length us, event | category | flops | bytes accessed | tf_op | source)
XLA Modules:
  0.0 31.9 jit_solution(14507762641725254512)
XLA Ops:
  0.0 30.4 %shard_map.64 = f32[48,768]{1,0:T(8,128)} custom-call(bf16[1536,1024]{1,0:T(8,128)(2,1)} %acts.1, bf16[1536,1024]{1,0:T(8,128)(2,1)} %grads.1, bf16[64,1024]{1,0:T(8,128)(2,1)} %bitcast.2, bf16[64,1024]{1,0:T(8,128)(2,1)} %bitcast.3, s32[24]{0:T(128)} %lengths.1, bf16[768,4096]{1,0:T(8,128)(2,1)} %stored.1), custom_call_target="tpu_custom_call" | custom-call | flops 704643072 | bytes 12730368 | tf_op jit(solution)/shard_map/pallas_call | solution.py:257
  30.4 1.6 %copy.8 = f32[48,768]{1,0:T(8,128)} copy(f32[48,768]{1,0:T(8,128)} %shard_map.64) | data formatting | bytes 294912

commit v4 on v2

--- a/solution.py
+++ b/solution.py
@@ -39,7 +39,7 @@
     feat, stores, slots_per_doc,
     acts, grads, in_basis, grad_basis, lengths, stored, scores,
     acts_v, grads_v, in_basis_v, grad_basis_v, stored_v, partial,
-    pair_out, pair_in, line_out, line_in, gathered, wide, queries,
+    pair_out, pair_in, line_out, line_in, gathered, wide, queries, sums,
     acts_sem, grads_sem, basis_sem, stored_sem,
     pair_send, pair_recv, line_send, line_recv, all_send, all_recv, core_send, core_recv,
 ):
@@ -91,15 +91,17 @@
     grad_wide = lax.dot_general(grad_basis_v[...], grad_place, over_rank, preferred_element_type=jnp.float32)
     in_wide, grad_wide = in_wide.astype(jnp.bfloat16), grad_wide.astype(jnp.bfloat16)
 
+    def project(step, half):
+        rows = pl.ds(pl.multiple_of(half * block, block), block)
+        return jnp.dot(acts_v[step, rows, :], in_wide, preferred_element_type=jnp.float32) + jnp.dot(
+            grads_v[step, rows, :], grad_wide, preferred_element_type=jnp.float32
+        )
+
     pair_copies = {}
     for index, step in enumerate(order):
         for load in loads[step]:
             load.wait()
-        partial[step] = jnp.dot(acts_v[step], in_wide, preferred_element_type=jnp.float32) + jnp.dot(
-            grads_v[step], grad_wide, preferred_element_type=jnp.float32
-        )
-        theirs = pl.ds(pl.multiple_of(other * block, block), block)
-        encode(pair_out.at[step], partial[step, theirs, :])
+        encode(pair_out.at[step], project(step, other))
         if index == 0:
             pl.semaphore_wait(barrier, feat - 1 + stores - 1)
         pair_copies[step] = remote(
@@ -115,12 +117,13 @@
         load.start()
         stored_loads.append(load)
 
-    mine = pl.ds(pl.multiple_of(my_pair * block, block), block)
+    for step in order:
+        partial[step] = project(step, my_pair)
     line_copies = {}
     total = None
     for step in order:
         pair_copies[step].wait_recv()
-        both = partial[step, mine, :] + decode(pair_in.at[step], block)
+        both = partial[step] + decode(pair_in.at[step], block)
         if step == 0:
             total = both
         else:
@@ -137,7 +140,6 @@
 
     position = lax.broadcasted_iota(jnp.int32, (slots_per_doc, rank), 0)
     left = lax.broadcasted_iota(jnp.int32, (slots_per_doc, LANES), 1) < rank
-    slot = core * feat + me
     for doc in range(docs):
         length = lengths[me * docs + doc]
         rows = total[doc * slots_per_doc:(doc + 1) * slots_per_doc]
@@ -150,60 +152,58 @@
         query = jnp.where(left[:pairs], outer[:pairs], outer[pairs:]) / length.astype(jnp.float32)
         query = query.astype(jnp.bfloat16)
         for part in range(HALVES):
-            gathered[part, slot, pl.ds(doc * part_rows, part_rows), :] = query[part * part_rows:(part + 1) * part_rows]
+            gathered[part, core, me, pl.ds(doc * part_rows, part_rows), :] = query[part * part_rows:(part + 1) * part_rows]
 
     sent = []
     for part in range(HALVES):
-        own = gathered.at[part, slot]
-        for shift in range(1, stores):
-            sent.append(remote(
-                own, own, core_send.at[part, shift, 0], core_recv.at[part, shift, 0],
-                {"store": lax.rem(core + shift, stores)},
-            ))
-            sent[-1].start()
+        own = gathered.at[part, core, me]
         for shift in range(1, feat):
             sent.append(remote(
                 own, own, all_send.at[part, shift], all_recv.at[part, shift], {"feat": lax.rem(me + shift, feat)}
             ))
             sent[-1].start()
-
-    wide_rows = wide.shape[0]
-    all_docs = queries.shape[0]
-    tile = 256
     for part in range(HALVES):
         for shift in range(1, feat):
-            source = core * feat + lax.rem(me + feat - shift, feat)
-            there = gathered.at[part, source]
+            there = gathered.at[part, core, lax.rem(me + feat - shift, feat)]
             remote(
                 there, there, all_send.at[part, shift], all_recv.at[part, shift], {"feat": lax.rem(me + shift, feat)}
             ).wait_recv()
-            for hop in range(1, stores):
-                sent.append(remote(
-                    there, there, core_send.at[part, hop, shift], core_recv.at[part, hop, shift],
-                    {"store": lax.rem(core + hop, stores)},
-                ))
-                sent[-1].start()
+        blocks = gathered.at[part, core]
         for hop in range(1, stores):
-            from_core = lax.rem(core + stores - hop, stores)
-            for shift in range(feat):
-                there = gathered.at[part, from_core * feat + lax.rem(me + feat - shift, feat)]
-                remote(
-                    there, there, core_send.at[part, hop, shift], core_recv.at[part, hop, shift],
-                    {"store": lax.rem(core + hop, stores)},
-                ).wait_recv()
+            sent.append(remote(
+                blocks, blocks, core_send.at[part, hop], core_recv.at[part, hop],
+                {"store": lax.rem(core + hop, stores)},
+            ))
+            sent[-1].start()
+
+    wide_rows = wide.shape[0]
+    all_docs = scores.shape[0]
+    queries[...] = jnp.zeros_like(queries)
+    tile = 256
+    for part in range(HALVES):
+        for hop in range(1, stores):
+            blocks = gathered.at[part, lax.rem(core + stores - hop, stores)]
+            remote(
+                blocks, blocks, core_send.at[part, hop], core_recv.at[part, hop],
+                {"store": lax.rem(core + hop, stores)},
+            ).wait_recv()
         wide[...] = gathered[part].reshape(wide_rows, LANES).astype(jnp.float32)
         for pair in range(part_rows):
-            queries[:, pair * LANES:(pair + 1) * LANES] = wide[pl.ds(pair, all_docs, part_rows), :].astype(jnp.bfloat16)
+            queries[:all_docs, pair * LANES:(pair + 1) * LANES] = wide[pl.ds(pair, all_docs, part_rows), :].astype(
+                jnp.bfloat16
+            )
         stored_loads[part].wait()
         for start in range(0, stored.shape[0], tile):
             product = lax.dot_general(
-                queries[...], stored_v[part, start:start + tile, :], (((1,), (1,)), ((), ())),
+                stored_v[part, start:start + tile, :], queries[...], (((1,), (1,)), ((), ())),
                 preferred_element_type=jnp.float32,
             )
-            if part == 0:
-                scores[:, start:start + tile] = product
+            if part:
+                product = product + sums[start:start + tile]
+            if part + 1 < HALVES:
+                sums[start:start + tile] = product
             else:
-                scores[:, start:start + tile] += product
+                scores[:, start:start + tile] = product.T[:all_docs]
 
     for step in order:
         pair_copies[step].wait_send()
@@ -219,6 +219,7 @@
     rank = input_basis.shape[1]
     rows, depth = stored_grads.shape
     docs = lengths.shape[0] * stores
+    padded = -(-docs // LANES) * LANES
     line = feat // PAIR
     block = tokens // feat
     part_rows = rank * rank // LANES // HALVES
@@ -237,18 +238,19 @@
             pltpu.VMEM((rank, features), bf16),
             pltpu.VMEM((rank, features), bf16),
             pltpu.VMEM((HALVES, rows, depth // HALVES), bf16),
-            pltpu.VMEM((line, PAIR * block, LANES), f32),
-            pltpu.VMEM((line, block + HEADER, LANES), jnp.int16),
-            pltpu.VMEM((line, block + HEADER, LANES), jnp.int16),
-            pltpu.VMEM((line, block + HEADER, LANES), jnp.int16),
-            pltpu.VMEM((line, block + HEADER, LANES), jnp.int16),
-            pltpu.VMEM((HALVES, stores * feat, share, LANES), bf16),
+            pltpu.VMEM((line, block, LANES), f32),
+            pltpu.VMEM((line, block + HEADER, LANES), jnp.int16),
+            pltpu.VMEM((line, block + HEADER, LANES), jnp.int16),
+            pltpu.VMEM((line, block + HEADER, LANES), jnp.int16),
+            pltpu.VMEM((line, block + HEADER, LANES), jnp.int16),
+            pltpu.VMEM((HALVES, stores, feat, share, LANES), bf16),
             pltpu.VMEM((docs * part_rows, LANES), f32),
-            pltpu.VMEM((docs, depth // HALVES), bf16),
+            pltpu.VMEM((padded, depth // HALVES), bf16),
+            pltpu.VMEM((rows, padded), f32),
             dma((line,)), dma((line,)), dma((2,)), dma((HALVES,)),
             dma((line,)), dma((line,)), dma((line,)), dma((line,)),
             dma((HALVES, feat)), dma((HALVES, feat)),
-            dma((HALVES, stores, feat)), dma((HALVES, stores, feat)),
+            dma((HALVES, stores)), dma((HALVES, stores)),
         ],
         compiler_params=pltpu.CompilerParams(
             collective_id=0, has_side_effects=True, vmem_limit_bytes=56 * 1024 * 1024

time: 29.6 us -> 27.1 us (0.916)
  Pallas kernels: 27.8 us -> 25.3 us
    pallas_call x1, Pallas kernels: 27.8 us -> 25.3 us  [per_device(): pl.pallas_call(functools.partial(kernel, feat, stores, slots_per_doc), ou...]
where the time goes in v4:
time: 27.1 us; the launch traced here: 26.9 us
  Pallas kernels  25.3 us (93%)
  local copies, waits for them, and re-layouts  1.58 us (6%)
    pallas_call x1, Pallas kernels, per_device(): pl.pallas_call(functools.partial(kernel, feat, stores, slots_per_doc), ou...  25.3 us
    unnamed x1, local copies, waits for them, and re-layouts  1.58 us

profile of v4, /device:TPU:0, one launch (start us, length us, event | category | flops | bytes accessed | tf_op | source)
XLA Modules:
  0.0 26.9 jit_solution(16410715847704906516)
XLA Ops:
  0.0 25.3 %shard_map.64 = f32[48,768]{1,0:T(8,128)} custom-call(bf16[1536,1024]{1,0:T(8,128)(2,1)} %acts.1, bf16[1536,1024]{1,0:T(8,128)(2,1)} %grads.1, bf16[64,1024]{1,0:T(8,128)(2,1)} %bitcast.2, bf16[64,1024]{1,0:T(8,128)(2,1)} %bitcast.3, s32[24]{0:T(128)} %lengths.1, bf16[768,4096]{1,0:T(8,128)(2,1)} %stored.1), custom_call_target="tpu_custom_call" | custom-call | flops 704643072 | bytes 12730368 | tf_op jit(solution)/shard_map/pallas_call | solution.py:230
  25.3 1.6 %copy.8 = f32[48,768]{1,0:T(8,128)} copy(f32[48,768]{1,0:T(8,128)} %shard_map.64) | data formatting | bytes 294912

commit v5 on v4

--- a/solution.py
+++ b/solution.py
@@ -44,7 +44,7 @@
     pair_send, pair_recv, line_send, line_recv, all_send, all_recv, core_send, core_recv,
 ):
     line = feat // PAIR
-    block = acts_v.shape[1] // PAIR
+    block = acts_v.shape[2]
     docs = block // slots_per_doc
     rank = in_basis.shape[0]
     pairs = rank * rank // LANES
@@ -56,6 +56,12 @@
     my_line, my_pair = me // PAIR, lax.rem(me, PAIR)
     other = 1 - my_pair
     twin = my_line * PAIR + other
+
+    barrier = pltpu.get_barrier_semaphore()
+    for shift in range(1, feat):
+        pl.semaphore_signal(barrier, inc=1, device_id={"feat": lax.rem(me + shift, feat)}, device_id_type=MESH)
+    for shift in range(1, stores):
+        pl.semaphore_signal(barrier, inc=1, device_id={"store": lax.rem(core + shift, stores)}, device_id_type=MESH)
 
     basis_loads = [
         pltpu.make_async_copy(in_basis, in_basis_v, basis_sem.at[0]),
@@ -64,21 +70,16 @@
     for load in basis_loads:
         load.start()
     loads = {}
-    for step in order:
-        spot = lax.rem(my_line + step, line)
-        rows = pl.ds(pl.multiple_of(spot * (PAIR * block), PAIR * block), PAIR * block)
-        loads[step] = [
-            pltpu.make_async_copy(acts.at[rows], acts_v.at[step], acts_sem.at[step]),
-            pltpu.make_async_copy(grads.at[rows], grads_v.at[step], grads_sem.at[step]),
-        ]
-        for load in loads[step]:
-            load.start()
-
-    barrier = pltpu.get_barrier_semaphore()
-    for shift in range(1, feat):
-        pl.semaphore_signal(barrier, inc=1, device_id={"feat": lax.rem(me + shift, feat)}, device_id_type=MESH)
-    for shift in range(1, stores):
-        pl.semaphore_signal(barrier, inc=1, device_id={"store": lax.rem(core + shift, stores)}, device_id_type=MESH)
+    for side, half in enumerate((other, my_pair)):
+        for step in order:
+            spot = lax.rem(my_line + step, line)
+            rows = pl.ds(pl.multiple_of((spot * PAIR + half) * block, block), block)
+            loads[side, step] = [
+                pltpu.make_async_copy(acts.at[rows], acts_v.at[side, step], acts_sem.at[side, step]),
+                pltpu.make_async_copy(grads.at[rows], grads_v.at[side, step], grads_sem.at[side, step]),
+            ]
+            for load in loads[side, step]:
+                load.start()
 
     row = lax.broadcasted_iota(jnp.int32, (rank, LANES), 0)
     lane = lax.broadcasted_iota(jnp.int32, (rank, LANES), 1)
@@ -91,17 +92,16 @@
     grad_wide = lax.dot_general(grad_basis_v[...], grad_place, over_rank, preferred_element_type=jnp.float32)
     in_wide, grad_wide = in_wide.astype(jnp.bfloat16), grad_wide.astype(jnp.bfloat16)
 
-    def project(step, half):
-        rows = pl.ds(pl.multiple_of(half * block, block), block)
-        return jnp.dot(acts_v[step, rows, :], in_wide, preferred_element_type=jnp.float32) + jnp.dot(
-            grads_v[step, rows, :], grad_wide, preferred_element_type=jnp.float32
+    def project(side, step):
+        for load in loads[side, step]:
+            load.wait()
+        return jnp.dot(acts_v[side, step], in_wide, preferred_element_type=jnp.float32) + jnp.dot(
+            grads_v[side, step], grad_wide, preferred_element_type=jnp.float32
         )
 
     pair_copies = {}
     for index, step in enumerate(order):
-        for load in loads[step]:
-            load.wait()
-        encode(pair_out.at[step], project(step, other))
+        encode(pair_out.at[step], project(0, step))
         if index == 0:
             pl.semaphore_wait(barrier, feat - 1 + stores - 1)
         pair_copies[step] = remote(
@@ -109,6 +109,7 @@
         )
         pair_copies[step].start()
 
+    queries[...] = jnp.zeros_like(queries)
     half = stored.shape[1] // HALVES
     stored_loads = []
     for part in range(HALVES):
@@ -118,7 +119,7 @@
         stored_loads.append(load)
 
     for step in order:
-        partial[step] = project(step, my_pair)
+        partial[step] = project(1, step)
     line_copies = {}
     total = None
     for step in order:
@@ -145,9 +146,12 @@
         rows = total[doc * slots_per_doc:(doc + 1) * slots_per_doc]
         grad_side = jnp.where(position < length, rows[:, :rank], 0.0)
         in_side = jnp.where(left, pltpu.roll(rows, rank, 1), rows)
+        grad_high, in_high = grad_side.astype(jnp.bfloat16), in_side.astype(jnp.bfloat16)
+        grad_low = (grad_side - grad_high.astype(jnp.float32)).astype(jnp.bfloat16)
+        in_low = (in_side - in_high.astype(jnp.float32)).astype(jnp.bfloat16)
         outer = lax.dot_general(
-            grad_side, in_side, (((0,), (0,)), ((), ())),
-            precision=lax.Precision.HIGHEST, preferred_element_type=jnp.float32,
+            jnp.concatenate([grad_high, grad_high, grad_low]), jnp.concatenate([in_high, in_low, in_high]),
+            (((0,), (0,)), ((), ())), preferred_element_type=jnp.float32,
         )
         query = jnp.where(left[:pairs], outer[:pairs], outer[pairs:]) / length.astype(jnp.float32)
         query = query.astype(jnp.bfloat16)
@@ -176,34 +180,43 @@
             ))
             sent[-1].start()
 
-    wide_rows = wide.shape[0]
-    all_docs = scores.shape[0]
-    queries[...] = jnp.zeros_like(queries)
+    core_docs = scores.shape[0] // stores
+    span = queries.shape[1] // stores
+
+    def lay_out(part, source, place):
+        wide[...] = gathered[part, source].reshape(wide.shape).astype(jnp.float32)
+        for pair in range(part_rows):
+            queries[part, place * span:place * span + core_docs, pair * LANES:(pair + 1) * LANES] = wide[
+                pl.ds(pair, core_docs, part_rows), :
+            ].astype(jnp.bfloat16)
+
+    for part in range(HALVES):
+        lay_out(part, core, 0)
     tile = 256
     for part in range(HALVES):
         for hop in range(1, stores):
-            blocks = gathered.at[part, lax.rem(core + stores - hop, stores)]
+            source = lax.rem(core + stores - hop, stores)
+            blocks = gathered.at[part, source]
             remote(
                 blocks, blocks, core_send.at[part, hop], core_recv.at[part, hop],
                 {"store": lax.rem(core + hop, stores)},
             ).wait_recv()
-        wide[...] = gathered[part].reshape(wide_rows, LANES).astype(jnp.float32)
-        for pair in range(part_rows):
-            queries[:all_docs, pair * LANES:(pair + 1) * LANES] = wide[pl.ds(pair, all_docs, part_rows), :].astype(
-                jnp.bfloat16
-            )
+            lay_out(part, source, hop)
         stored_loads[part].wait()
         for start in range(0, stored.shape[0], tile):
             product = lax.dot_general(
-                stored_v[part, start:start + tile, :], queries[...], (((1,), (1,)), ((), ())),
+                stored_v[part, start:start + tile, :], queries[part], (((1,), (1,)), ((), ())),
                 preferred_element_type=jnp.float32,
             )
             if part:
                 product = product + sums[start:start + tile]
             if part + 1 < HALVES:
                 sums[start:start + tile] = product
-            else:
-                scores[:, start:start + tile] = product.T[:all_docs]
+                continue
+            turned = product.T
+            for hop in range(stores):
+                rows = pl.ds(pl.multiple_of(lax.rem(core + stores - hop, stores) * core_docs, core_docs), core_docs)
+                scores[rows, start:start + tile] = turned[hop * span:hop * span + core_docs]
 
     for step in order:
         pair_copies[step].wait_send()
@@ -233,8 +246,8 @@
         in_specs=[anywhere] * 4 + [pl.BlockSpec(memory_space=pltpu.SMEM), anywhere],
         out_specs=pl.BlockSpec(memory_space=pltpu.VMEM),
         scratch_shapes=[
-            pltpu.VMEM((line, PAIR * block, features), bf16),
-            pltpu.VMEM((line, PAIR * block, features), bf16),
+            pltpu.VMEM((2, line, block, features), bf16),
+            pltpu.VMEM((2, line, block, features), bf16),
             pltpu.VMEM((rank, features), bf16),
             pltpu.VMEM((rank, features), bf16),
             pltpu.VMEM((HALVES, rows, depth // HALVES), bf16),
@@ -244,16 +257,16 @@
             pltpu.VMEM((line, block + HEADER, LANES), jnp.int16),
             pltpu.VMEM((line, block + HEADER, LANES), jnp.int16),
             pltpu.VMEM((HALVES, stores, feat, share, LANES), bf16),
-            pltpu.VMEM((docs * part_rows, LANES), f32),
-            pltpu.VMEM((padded, depth // HALVES), bf16),
+            pltpu.VMEM((docs // stores * part_rows, LANES), f32),
+            pltpu.VMEM((HALVES, padded, depth // HALVES), bf16),
             pltpu.VMEM((rows, padded), f32),
-            dma((line,)), dma((line,)), dma((2,)), dma((HALVES,)),
+            dma((2, line)), dma((2, line)), dma((2,)), dma((HALVES,)),
             dma((line,)), dma((line,)), dma((line,)), dma((line,)),
             dma((HALVES, feat)), dma((HALVES, feat)),
             dma((HALVES, stores)), dma((HALVES, stores)),
         ],
         compiler_params=pltpu.CompilerParams(
-            collective_id=0, has_side_effects=True, vmem_limit_bytes=56 * 1024 * 1024
+            collective_id=0, has_side_effects=True, vmem_limit_bytes=53 * 1024 * 1024
         ),
         cost_estimate=pl.CostEstimate(
             flops=4 * tokens * features * rank + 2 * docs * rows * depth,

time: 27.1 us -> 28.1 us (1.037)
  local copies, waits for them, and re-layouts: 1.58 us -> 3.13 us
  Pallas kernels: 25.3 us -> 24.8 us
    unnamed x1 -> x7, local copies, waits for them, and re-layouts: 1.58 us -> 3.13 us
    pallas_call x1, Pallas kernels: 25.3 us -> 24.8 us  [per_device(): pl.pallas_call(functools.partial(kernel, feat, stores, slots_per_doc), ou...]
where the time goes in v5:
time: 28.1 us; the launch traced here: 28 us
  Pallas kernels  24.8 us (88%)
  local copies, waits for them, and re-layouts  3.13 us (11%)
    pallas_call x1, Pallas kernels, per_device(): pl.pallas_call(functools.partial(kernel, feat, stores, slots_per_doc), ou...  24.8 us
    unnamed x7, local copies, waits for them, and re-layouts  3.13 us

profile of v5, /device:TPU:0, one launch (start us, length us, event | category | flops | bytes accessed | tf_op | source)
XLA Modules:
  0.0 28.0 jit_solution(17543934429482094010)
XLA Ops:
  0.0 0.0 copy-start
  0.0 0.9 %copy-done = bf16[1024,64]{0,1:T(8,128)(2,1)S(1)} copy-done((bf16[1024,64]{0,1:T(8,128)(2,1)S(1)}, bf16[1024,64]{0,1:T(8,128)(2,1)}, u32[]{:S(2)}) %copy-start) | copy-done | bytes 131096
  0.9 0.0 copy-start.1
  0.9 0.9 %copy-done.1 = bf16[1024,64]{0,1:T(8,128)(2,1)S(1)} copy-done((bf16[1024,64]{0,1:T(8,128)(2,1)S(1)}, bf16[1024,64]{0,1:T(8,128)(2,1)}, u32[]{:S(2)}) %copy-start.1) | copy-done | bytes 131096
  1.8 0.0 copy-start.2
  1.8 0.7 %copy-done.2 = s32[24]{0:T(128)S(1)} copy-done((s32[24]{0:T(128)S(1)}, s32[24]{0:T(128)}, u32[]{:S(2)}) %copy-start.2) | copy-done | bytes 120
  2.5 24.8 %shard_map.64 = f32[48,768]{1,0:T(8,128)S(1)} custom-call(bf16[1536,1024]{1,0:T(8,128)(2,1)} %acts.1, bf16[1536,1024]{1,0:T(8,128)(2,1)} %grads.1, bf16[64,1024]{1,0:T(8,128)(2,1)S(1)} %bitcast.2, bf16[64,1024]{1,0:T(8,128)(2,1)S(1)} %bitcast.3, s32[24]{0:T(128)S(1)} %copy-done.2, bf16[768,4096]{1,0:T(8,128)(2,1)} %stored.1), custom_call_target="tpu_custom_call" | custom-call | flops 704643072 | bytes 12730368 | tf_op jit(solution)/shard_map/pallas_call | solution.py:243
  27.3 0.7 %copy.8 = f32[48,768]{1,0:T(8,128)} copy(f32[48,768]{1,0:T(8,128)S(1)} %shard_map.64) | data formatting | bytes 294912
Async XLA Ops:
  0.0 0.9 %copy-start = (bf16[1024,64]{0,1:T(8,128)(2,1)S(1)}, bf16[1024,64]{0,1:T(8,128)(2,1)}, u32[]{:S(2)}) copy-start(bf16[1024,64]{0,1:T(8,128)(2,1)} %param.8) | copy-start | bytes 393220
  0.9 0.9 %copy-start.1 = (bf16[1024,64]{0,1:T(8,128)(2,1)S(1)}, bf16[1024,64]{0,1:T(8,128)(2,1)}, u32[]{:S(2)}) copy-start(bf16[1024,64]{0,1:T(8,128)(2,1)} %param.9) | copy-start | bytes 393220
  1.8 0.7 %copy-start.2 = (s32[24]{0:T(128)S(1)}, s32[24]{0:T(128)}, u32[]{:S(2)}) copy-start(s32[24]{0:T(128)} %lengths.1) | copy-start | bytes 292

commit v6 on v5

--- a/solution.py
+++ b/solution.py
@@ -38,9 +38,9 @@
 def kernel(
     feat, stores, slots_per_doc,
     acts, grads, in_basis, grad_basis, lengths, stored, scores,
-    acts_v, grads_v, in_basis_v, grad_basis_v, stored_v, partial,
+    acts_v, grads_v, in_basis_v, grad_basis_v, lengths_s, stored_v, partial,
     pair_out, pair_in, line_out, line_in, gathered, wide, queries, sums,
-    acts_sem, grads_sem, basis_sem, stored_sem,
+    acts_sem, grads_sem, basis_sem, lengths_sem, stored_sem,
     pair_send, pair_recv, line_send, line_recv, all_send, all_recv, core_send, core_recv,
 ):
     line = feat // PAIR
@@ -110,6 +110,8 @@
         pair_copies[step].start()
 
     queries[...] = jnp.zeros_like(queries)
+    lengths_load = pltpu.make_async_copy(lengths, lengths_s, lengths_sem)
+    lengths_load.start()
     half = stored.shape[1] // HALVES
     stored_loads = []
     for part in range(HALVES):
@@ -139,10 +141,11 @@
         line_copies[step].wait_recv()
         total = total + decode(line_in.at[step], block)
 
+    lengths_load.wait()
     position = lax.broadcasted_iota(jnp.int32, (slots_per_doc, rank), 0)
     left = lax.broadcasted_iota(jnp.int32, (slots_per_doc, LANES), 1) < rank
     for doc in range(docs):
-        length = lengths[me * docs + doc]
+        length = lengths_s[me * docs + doc]
         rows = total[doc * slots_per_doc:(doc + 1) * slots_per_doc]
         grad_side = jnp.where(position < length, rows[:, :rank], 0.0)
         in_side = jnp.where(left, pltpu.roll(rows, rank, 1), rows)
@@ -242,14 +245,15 @@
     anywhere = pl.BlockSpec(memory_space=pl.ANY)
     return pl.pallas_call(
         functools.partial(kernel, feat, stores, slots_per_doc),
-        out_shape=jax.ShapeDtypeStruct((docs, rows), f32),
-        in_specs=[anywhere] * 4 + [pl.BlockSpec(memory_space=pltpu.SMEM), anywhere],
+        out_shape=pltpu.VMEM((docs, rows), f32),
+        in_specs=[anywhere] * 6,
         out_specs=pl.BlockSpec(memory_space=pltpu.VMEM),
         scratch_shapes=[
             pltpu.VMEM((2, line, block, features), bf16),
             pltpu.VMEM((2, line, block, features), bf16),
             pltpu.VMEM((rank, features), bf16),
             pltpu.VMEM((rank, features), bf16),
+            pltpu.SMEM(lengths.shape, jnp.int32),
             pltpu.VMEM((HALVES, rows, depth // HALVES), bf16),
             pltpu.VMEM((line, block, LANES), f32),
             pltpu.VMEM((line, block + HEADER, LANES), jnp.int16),
@@ -260,7 +264,7 @@
             pltpu.VMEM((docs // stores * part_rows, LANES), f32),
             pltpu.VMEM((HALVES, padded, depth // HALVES), bf16),
             pltpu.VMEM((rows, padded), f32),
-            dma((2, line)), dma((2, line)), dma((2,)), dma((HALVES,)),
+            dma((2, line)), dma((2, line)), dma((2,)), dma(()), dma((HALVES,)),
             dma((line,)), dma((line,)), dma((line,)), dma((line,)),
             dma((HALVES, feat)), dma((HALVES, feat)),
             dma((HALVES, stores)), dma((HALVES, stores)),
@@ -273,7 +277,10 @@
             bytes_accessed=4 * tokens * features + 2 * rows * depth + 4 * docs * rows,
             transcendentals=0,
         ),
-    )(activations, output_grads, input_basis.T, grad_basis.T, lengths, stored_grads)
+    )(*[
+        pltpu.with_memory_space_constraint(operand, pltpu.HBM)
+        for operand in (activations, output_grads, input_basis.T, grad_basis.T, lengths, stored_grads)
+    ])
 
 
 def solution(mesh):

time: 28.1 us -> 25.1 us (0.89)
  local copies, waits for them, and re-layouts: 3.13 us -> 0.66 us
  Pallas kernels: 24.8 us -> 24.3 us
    unnamed x7 -> x1, local copies, waits for them, and re-layouts: 3.13 us -> 0.66 us
    pallas_call x1, Pallas kernels: 24.8 us -> 24.3 us  [per_device(): pl.pallas_call(functools.partial(kernel, feat, stores, slots_per_doc), ou...]
where the time goes in v6:
time: 25.1 us; the launch traced here: 25 us
  Pallas kernels  24.3 us (97%)
  local copies, waits for them, and re-layouts  0.66 us (3%)
    pallas_call x1, Pallas kernels, per_device(): pl.pallas_call(functools.partial(kernel, feat, stores, slots_per_doc), ou...  24.3 us
    unnamed x1, local copies, waits for them, and re-layouts  0.66 us

profile of v6, /device:TPU:0, one launch (start us, length us, event | category | flops | bytes accessed | tf_op | source)
XLA Modules:
  0.0 25.0 jit_solution(2229143977472062255)
XLA Ops:
  0.0 24.3 %shard_map.64 = f32[48,768]{1,0:T(8,128)S(1)} custom-call(bf16[1536,1024]{1,0:T(8,128)(2,1)} %acts.1, bf16[1536,1024]{1,0:T(8,128)(2,1)} %grads.1, bf16[64,1024]{1,0:T(8,128)(2,1)} %bitcast.2, bf16[64,1024]{1,0:T(8,128)(2,1)} %bitcast.3, s32[24]{0:T(128)} %lengths.1, bf16[768,4096]{1,0:T(8,128)(2,1)} %stored.1), custom_call_target="tpu_custom_call" | custom-call | flops 704643072 | bytes 12730368 | tf_op jit(solution)/shard_map/pallas_call | solution.py:246
  24.3 0.7 %copy.8 = f32[48,768]{1,0:T(8,128)} copy(f32[48,768]{1,0:T(8,128)S(1)} %shard_map.64) | data formatting | bytes 294912

commit v7 on v6

--- a/solution.py
+++ b/solution.py
@@ -11,6 +11,7 @@
 PAIR = 2
 HALVES = 2
 LANES = 128
+AHEAD = 3
 HEADER = 16
 
 
@@ -38,7 +39,7 @@
 def kernel(
     feat, stores, slots_per_doc,
     acts, grads, in_basis, grad_basis, lengths, stored, scores,
-    acts_v, grads_v, in_basis_v, grad_basis_v, lengths_s, stored_v, partial,
+    acts_v, grads_v, in_basis_v, grad_basis_v, lengths_s, stored_v,
     pair_out, pair_in, line_out, line_in, gathered, wide, queries, sums,
     acts_sem, grads_sem, basis_sem, lengths_sem, stored_sem,
     pair_send, pair_recv, line_send, line_recv, all_send, all_recv, core_send, core_recv,
@@ -56,12 +57,6 @@
     my_line, my_pair = me // PAIR, lax.rem(me, PAIR)
     other = 1 - my_pair
     twin = my_line * PAIR + other
-
-    barrier = pltpu.get_barrier_semaphore()
-    for shift in range(1, feat):
-        pl.semaphore_signal(barrier, inc=1, device_id={"feat": lax.rem(me + shift, feat)}, device_id_type=MESH)
-    for shift in range(1, stores):
-        pl.semaphore_signal(barrier, inc=1, device_id={"store": lax.rem(core + shift, stores)}, device_id_type=MESH)
 
     basis_loads = [
         pltpu.make_async_copy(in_basis, in_basis_v, basis_sem.at[0]),
@@ -78,8 +73,21 @@
                 pltpu.make_async_copy(acts.at[rows], acts_v.at[side, step], acts_sem.at[side, step]),
                 pltpu.make_async_copy(grads.at[rows], grads_v.at[side, step], grads_sem.at[side, step]),
             ]
-            for load in loads[side, step]:
+    waiting = list(loads.values())
+
+    def start_next():
+        if waiting:
+            for load in waiting.pop(0):
                 load.start()
+
+    for _ in range(AHEAD):
+        start_next()
+
+    barrier = pltpu.get_barrier_semaphore()
+    for shift in range(1, feat):
+        pl.semaphore_signal(barrier, inc=1, device_id={"feat": lax.rem(me + shift, feat)}, device_id_type=MESH)
+    for shift in range(1, stores):
+        pl.semaphore_signal(barrier, inc=1, device_id={"store": lax.rem(core + shift, stores)}, device_id_type=MESH)
 
     row = lax.broadcasted_iota(jnp.int32, (rank, LANES), 0)
     lane = lax.broadcasted_iota(jnp.int32, (rank, LANES), 1)
@@ -95,6 +103,7 @@
     def project(side, step):
         for load in loads[side, step]:
             load.wait()
+        start_next()
         return jnp.dot(acts_v[side, step], in_wide, preferred_element_type=jnp.float32) + jnp.dot(
             grads_v[side, step], grad_wide, preferred_element_type=jnp.float32
         )
@@ -120,13 +129,12 @@
         load.start()
         stored_loads.append(load)
 
-    for step in order:
-        partial[step] = project(1, step)
     line_copies = {}
     total = None
     for step in order:
+        own_half = project(1, step)
         pair_copies[step].wait_recv()
-        both = partial[step] + decode(pair_in.at[step], block)
+        both = own_half + decode(pair_in.at[step], block)
         if step == 0:
             total = both
         else:
@@ -255,7 +263,6 @@
             pltpu.VMEM((rank, features), bf16),
             pltpu.SMEM(lengths.shape, jnp.int32),
             pltpu.VMEM((HALVES, rows, depth // HALVES), bf16),
-            pltpu.VMEM((line, block, LANES), f32),
             pltpu.VMEM((line, block + HEADER, LANES), jnp.int16),
             pltpu.VMEM((line, block + HEADER, LANES), jnp.int16),
             pltpu.VMEM((line, block + HEADER, LANES), jnp.int16),

time: 25.1 us -> 25.2 us (level)
  no operation moved by 1% of the time
where the time goes in v7:
time: 25.2 us; the launch traced here: 25 us
  Pallas kernels  24.3 us (96%)
  local copies, waits for them, and re-layouts  0.66 us (3%)
    pallas_call x1, Pallas kernels, per_device(): pl.pallas_call(functools.partial(kernel, feat, stores, slots_per_doc), ou...  24.3 us
    unnamed x1, local copies, waits for them, and re-layouts  0.66 us

profile of v7, /device:TPU:0, one launch (start us, length us, event | category | flops | bytes accessed | tf_op | source)
XLA Modules:
  0.0 25.0 jit_solution(9481351872516266911)
XLA Ops:
  0.0 24.3 %shard_map.64 = f32[48,768]{1,0:T(8,128)S(1)} custom-call(bf16[1536,1024]{1,0:T(8,128)(2,1)} %acts.1, bf16[1536,1024]{1,0:T(8,128)(2,1)} %grads.1, bf16[64,1024]{1,0:T(8,128)(2,1)} %bitcast.2, bf16[64,1024]{1,0:T(8,128)(2,1)} %bitcast.3, s32[24]{0:T(128)} %lengths.1, bf16[768,4096]{1,0:T(8,128)(2,1)} %stored.1), custom_call_target="tpu_custom_call" | custom-call | flops 704643072 | bytes 12730368 | tf_op jit(solution)/shard_map/pallas_call | solution.py:254
  24.4 0.7 %copy.8 = f32[48,768]{1,0:T(8,128)} copy(f32[48,768]{1,0:T(8,128)S(1)} %shard_map.64) | data formatting | bytes 294912

commit v8 on v7

--- a/solution.py
+++ b/solution.py
@@ -177,6 +177,16 @@
                 own, own, all_send.at[part, shift], all_recv.at[part, shift], {"feat": lax.rem(me + shift, feat)}
             ))
             sent[-1].start()
+    core_docs = scores.shape[0] // stores
+    span = queries.shape[1] // stores
+
+    def lay_out(part, source, place):
+        wide[...] = gathered[part, source].reshape(wide.shape).astype(jnp.float32)
+        for pair in range(part_rows):
+            queries[part, place * span:place * span + core_docs, pair * LANES:(pair + 1) * LANES] = wide[
+                pl.ds(pair, core_docs, part_rows), :
+            ].astype(jnp.bfloat16)
+
     for part in range(HALVES):
         for shift in range(1, feat):
             there = gathered.at[part, core, lax.rem(me + feat - shift, feat)]
@@ -190,19 +200,8 @@
                 {"store": lax.rem(core + hop, stores)},
             ))
             sent[-1].start()
-
-    core_docs = scores.shape[0] // stores
-    span = queries.shape[1] // stores
-
-    def lay_out(part, source, place):
-        wide[...] = gathered[part, source].reshape(wide.shape).astype(jnp.float32)
-        for pair in range(part_rows):
-            queries[part, place * span:place * span + core_docs, pair * LANES:(pair + 1) * LANES] = wide[
-                pl.ds(pair, core_docs, part_rows), :
-            ].astype(jnp.bfloat16)
-
-    for part in range(HALVES):
         lay_out(part, core, 0)
+
     tile = 256
     for part in range(HALVES):
         for hop in range(1, stores):

time: 25.2 us -> 25.1 us (level)
  no operation moved by 1% of the time
where the time goes in v8:
time: 25.1 us; the launch traced here: 24.9 us
  Pallas kernels  24.3 us (97%)
  local copies, waits for them, and re-layouts  0.66 us (3%)
    pallas_call x1, Pallas kernels, per_device(): pl.pallas_call(functools.partial(kernel, feat, stores, slots_per_doc), ou...  24.3 us
    unnamed x1, local copies, waits for them, and re-layouts  0.66 us

profile of v8, /device:TPU:0, one launch (start us, length us, event | category | flops | bytes accessed | tf_op | source)
XLA Modules:
  0.0 24.9 jit_solution(9657023474708859292)
XLA Ops:
  0.0 24.3 %shard_map.64 = f32[48,768]{1,0:T(8,128)S(1)} custom-call(bf16[1536,1024]{1,0:T(8,128)(2,1)} %acts.1, bf16[1536,1024]{1,0:T(8,128)(2,1)} %grads.1, bf16[64,1024]{1,0:T(8,128)(2,1)} %bitcast.2, bf16[64,1024]{1,0:T(8,128)(2,1)} %bitcast.3, s32[24]{0:T(128)} %lengths.1, bf16[768,4096]{1,0:T(8,128)(2,1)} %stored.1), custom_call_target="tpu_custom_call" | custom-call | flops 704643072 | bytes 12730368 | tf_op jit(solution)/shard_map/pallas_call | solution.py:253
  24.3 0.7 %copy.8 = f32[48,768]{1,0:T(8,128)} copy(f32[48,768]{1,0:T(8,128)S(1)} %shard_map.64) | data formatting | bytes 294912
